TPU v7x, 32 devices: a whole 2x2x4 slice. The times are simulated.
32 devices in a mesh: bed: 8 (over y, x, core), layer: 4 (over z).
Axes of the slice: x: 2, y: 2, z: 4, core: 2. Of those that a mesh axis runs over, the one named last changes fastest.
Arguments:
- concentration: float32 [8, 1024, 4096], P('layer', 'bed'), may hold values from 0.2 to 2
- east_velocity: bfloat16 [8, 1024, 4096], P('layer', 'bed'), may hold values from -3 to 3
- north_velocity: bfloat16 [8, 1024, 4096], P('layer', 'bed'), may hold values from -3 to 3
- settling: float32 [1024, 4096], P('bed'), may hold values from 0.02 to 0.15
- surface: float32 [1024, 4096], P('bed'), may hold values from 1.8 to 6
- bed_level: float32 [1024, 4096], P('bed'), may hold values from -1 to 1
- erosion: float32 [1024, 4096], P('bed'), may hold values from 0 to 0.08
- wet_mask: int32 [1024, 4096], P('bed'), may hold values 0 or 1
Outputs:
- new_concentration: float32 [8, 1024, 4096], P('layer', 'bed')
- new_bed: float32 [1024, 4096], P('bed')
Inputs may be any that keep to these rules, and one draw needn't show every extreme that they name: `wet_mask`: 1 marks a wet cell, 0 a dry one.
All inputs are finite; a program needn't handle non-finite values. No bound on the sum of `wet_mask` on one device may be relied on, other than what follows from the above.
Results may differ from a plain program's by a relative error of at most 0.0003.
Values sent between devices are 32-bit elements; how exact they have to be, the bound alone decides.
A program may use at most 128 MiB of HBM per device.

v0:
```python
import jax
import jax.numpy as jnp
from jax import lax
from jax.sharding import PartitionSpec as P

SWEEPS = 4
ADVECT_RATE = 0.1
FLUX_GAIN = 0.15
POROSITY_GAIN = 1.0 / 0.6
RELAX_RATE = 0.2
CRIT_SLOPE = 0.5
DEPTH_FLOOR = 1.0


def padded(block, sides, width):
    for axis, dim in sides:
        count = lax.axis_size(axis)
        forward = [(i, i + 1) for i in range(count - 1)]
        backward = [(target, source) for source, target in forward]
        low = lax.ppermute(
            lax.slice_in_dim(block, block.shape[dim] - width, None, axis=dim), axis, forward
        )
        high = lax.ppermute(lax.slice_in_dim(block, 0, width, axis=dim), axis, backward)
        block = jnp.concatenate([low, block, high], axis=dim)
    return block


def passed_along(block, axis, distance):
    devices = range(lax.axis_size(axis))
    route = [(i - distance, i) for i in devices if i - distance in devices]
    return lax.ppermute(block, axis, route)


def face_divergence(values, speeds, which_axis):
    length_here = values.shape[which_axis]
    left_val = lax.slice_in_dim(values, 0, length_here - 1, axis=which_axis)
    right_val = lax.slice_in_dim(values, 1, length_here, axis=which_axis)
    left_spd = lax.slice_in_dim(speeds, 0, length_here - 1, axis=which_axis)
    right_spd = lax.slice_in_dim(speeds, 1, length_here, axis=which_axis)
    face_speed = 0.5 * (left_spd + right_spd)
    face_flux = jnp.maximum(face_speed, 0.0) * left_val + jnp.minimum(face_speed, 0.0) * right_val
    return lax.slice_in_dim(face_flux, 1, length_here - 1, axis=which_axis) - lax.slice_in_dim(
        face_flux, 0, length_here - 2, axis=which_axis
    )


def slide_sweep(height, wetness):
    drop_x = height[:-1, :] - height[1:, :]
    move_x = (
        RELAX_RATE
        * (drop_x - jnp.clip(drop_x, -CRIT_SLOPE, CRIT_SLOPE))
        * wetness[:-1, :]
        * wetness[1:, :]
    )
    drop_y = height[:, :-1] - height[:, 1:]
    move_y = (
        RELAX_RATE
        * (drop_y - jnp.clip(drop_y, -CRIT_SLOPE, CRIT_SLOPE))
        * wetness[:, :-1]
        * wetness[:, 1:]
    )
    return (
        height[1:-1, 1:-1]
        - move_x[1:, 1:-1]
        + move_x[:-1, 1:-1]
        - move_y[1:-1, 1:]
        + move_y[1:-1, :-1]
    )


def edge_pair(field):
    return jnp.concatenate([field[:, :1], field[:, -1:]], 1)


def body(
    concentration, east_velocity, north_velocity, settling, surface, bed_level, erosion, wet_mask
):
    layers_here = concentration.shape[0]
    layer_count = layers_here * lax.axis_size("layer")
    layer_index = lax.axis_index("layer")
    water_depth = surface - bed_level
    layer_thick = water_depth / layer_count
    east_speed = east_velocity.astype(jnp.float32)
    north_speed = north_velocity.astype(jnp.float32)
    flux_east = east_speed * concentration * layer_thick
    flux_north = north_speed * concentration * layer_thick
    edges = jnp.stack([edge_pair(concentration), edge_pair(east_speed), edge_pair(flux_east)])
    rims = padded(edges, (("bed", 2),), 1)
    before = rims[:, :, :1]
    after = rims[:, :, 3:]
    conc_along = jnp.concatenate([before[0], concentration, after[0]], 1)
    speed_along = jnp.concatenate([before[1], east_speed, after[1]], 1)
    east_wide = jnp.concatenate([before[2], flux_east, after[2]], 1)
    upper_row = passed_along(concentration[0], "layer", -1)
    pad_y = ((0, 0), (0, 0), (1, 1))
    advect = face_divergence(conc_along, speed_along, 1) + face_divergence(
        jnp.pad(concentration, pad_y), jnp.pad(north_speed, pad_y), 2
    )
    bottom_flag = (layer_index == 0).astype(jnp.float32)
    falling = jnp.concatenate([concentration[1:], upper_row[None]], 0) * settling
    source = falling - settling * concentration
    source = source.at[0].add(bottom_flag * erosion)
    settled = concentration - ADVECT_RATE * advect + layer_count / water_depth * source
    north_wide = jnp.pad(flux_north, pad_y)
    spread = 0.5 * (
        east_wide[:, 2:, :] - east_wide[:, :-2, :] + north_wide[:, :, 2:] - north_wide[:, :, :-2]
    )
    bed_change = FLUX_GAIN * jnp.sum(spread, 0) - bottom_flag * settling * concentration[0]
    wet_float = wet_mask.astype(jnp.float32)
    rim_width, rounds = (1, SWEEPS)
    summed_flux = lax.psum(bed_change, "layer")
    height = bed_level - POROSITY_GAIN * wet_float * (summed_flux + erosion)
    side_pad = ((0, 0), (rim_width, rim_width))
    wet_wide = jnp.pad(padded(wet_float, (("bed", 0),), rim_width), side_pad)
    for round_index in range(rounds):
        height_wide = jnp.pad(padded(height, (("bed", 0),), rim_width), side_pad)
        wetness = wet_wide
        height_wide = slide_sweep(height_wide, wetness)
        wetness = wetness[1:-1, 1:-1]
        height = height_wide
    new_depth = jnp.maximum(surface - height, DEPTH_FLOOR)
    return (settled * (water_depth / new_depth), height)


def solution(mesh):
    in_specs = (
        P("layer", "bed", None),
        P("layer", "bed", None),
        P("layer", "bed", None),
        P("bed", None),
        P("bed", None),
        P("bed", None),
        P("bed", None),
        P("bed", None),
    )
    out_specs = (P("layer", "bed", None), P("bed", None))
    return jax.shard_map(body, mesh=mesh, in_specs=in_specs, out_specs=out_specs, check_vma=False)
```

profile of v0, /device:TPU:4, one launch (start us, length us, event | category | flops | bytes accessed | tf_op | source)
XLA Modules:
  0.0 256.3 jit_solution(9465956623220491633)
XLA Ops:
  7.2 2.7 %fusion.39 = (f32[1,128,4096]{2,1,0:T(8,128)S(1)}, f32[128,4096]{1,0:T(8,128)S(1)}) fusion(f32[2,128,4096]{2,1,0:T(8,128)} %param.10), kind=kLoop, calls=%fused_computation.111 | loop fusion | bytes 8388608 | tf_op jit(solution)/shard_map/slice | solution.py:100
  11.9 3.4 %broadcast_divide_fusion = (f32[128,4096]{1,0:T(8,128)}, f32[128,4096]{1,0:T(8,128)S(1)}) fusion(f32[128,4096]{1,0:T(8,128)} %param.14, f32[128,4096]{1,0:T(8,128)S(1)} %copy-done.16), kind=kLoop, calls=%fused_computation.99 | loop fusion | flops 1048576 | bytes 8388608 | tf_op jit(solution)/shard_map/div | solution.py:103
  16.8 42.6 %collective-permute-done.2 = f32[128,4096]{1,0:T(8,128)S(1)} collective-permute-done((f32[128,4096]{1,0:T(8,128)S(1)}, f32[128,4096]{1,0:T(8,128)S(1)}, u32[]{:S(2)}, u32[]{:S(2)}) %collective-permute-start.2) | collective-permute-done | bytes 2097184 | tf_op jit(solution)/shard_map/ppermute | solution.py:31
  59.5 4.4 %multiply_multiply_fusion = (f32[2,128,4096]{2,1,0:T(8,128)}, f32[2,128,4096]{2,1,0:T(8,128)S(1)}, f32[2,128,4096]{2,1,0:T(8,128)}) fusion(f32[2,128,4096]{2,1,0:T(8,128)S(1)} %copy-done, f32[128,4096]{1,0:T(8,128)S(1)} %broadcast_multiply_fusion, bf16[2,128,4096]{2,1,0:T(8,128)(2,1)S(1)} %copy-done.11, bf16[2,128,4096]{2,1,0:T(8,128)(2,1)S(1)} %copy-done.8, ...), kind=kLoop, calls=%fused_computation.22 | loop fusion | flops 10485760 | bytes 29360128 | tf_op jit(solution)/shard_map/mul | solution.py:86
  68.2 2.4 collective-permute-start
  70.7 4.4 %collective-permute-done = f32[3,2,1,4096]{3,2,1,0:T(1,128)S(1)} collective-permute-done((f32[3,2,1,4096]{3,2,1,0:T(1,128)S(1)}, f32[3,2,1,4096]{3,2,1,0:T(1,128)S(1)}, u32[]{:S(2)}, u32[]{:S(2)}) %collective-permute-start) | collective-permute-done | bytes 98336 | tf_op jit(solution)/shard_map/ppermute | solution.py:20
  75.1 8.3 %fusion.6 = f32[128,4096]{1,0:T(8,128)S(1)} fusion(f32[2,128,4096]{2,1,0:T(8,128)} %copy-done.6, f32[2,1,4096]{2,1,0:T(1,128)S(1)} %get-tuple-element.44, f32[2,1,4096]{2,1,0:T(1,128)S(1)} %get-tuple-element.41, f32[2,128,4096]{2,1,0:T(8,128)} %get-tuple-element.18), kind=kLoop, calls=%fused_computation.11 | loop fusion | flops 6815744 | bytes 10551296 | tf_op jit(solution)/shard_map/reduce_sum | solution.py:108
  90.6 4.5 %collective-permute-start.6 = (f32[1,4096]{1,0:T(1,128)S(1)}, f32[1,4096]{1,0:T(1,128)S(1)}, u32[]{:S(2)}, u32[]{:S(2)}) collective-permute-start(f32[1,4096]{1,0:T(1,128)S(1)} %get-tuple-element.34), channel_id=1, source_target_pairs={{4,0},{8,4},{12,8},{16,12},{20,16},{24,20},{28,24},{5,1},{9,5},{13... | collective-permute-start | bytes 49160 | tf_op jit(solution)/shard_map/ppermute | solution.py:23
  95.1 2.5 convert_element_type.23
  97.6 73.6 %all-reduce.10.cloned.1.call-done = f32[128,4096]{1,0:T(8,128)} async-done(((f32[128,4096]{1,0:T(8,128)}), f32[128,4096]{1,0:T(8,128)}) %all-reduce.10.cloned.1.call-update) | async-done | bytes 2097168 | tf_op jit(solution)/shard_map/psum | solution.py:111
  171.2 4.2 %multiply_subtract_fusion = f32[128,4096]{1,0:T(8,128)S(1)} fusion(f32[128,4096]{1,0:T(8,128)} %param.15, f32[128,4096]{1,0:T(8,128)} %all-reduce.10.cloned.1.call-done, f32[128,4096]{1,0:T(8,128)} %param.16, s32[128,4096]{1,0:T(8,128)} %param.17), kind=kLoop, calls=%fused_computation.96 | loop fusion | flops 2621440 | bytes 10485760 | tf_op jit(solution)/shard_map/sub | solution.py:112
  177.4 4.5 %collective-permute-start.4 = (f32[1,4096]{1,0:T(1,128)S(1)}, f32[1,4096]{1,0:T(1,128)S(1)}, u32[]{:S(2)}, u32[]{:S(2)}) collective-permute-start(f32[1,4096]{1,0:T(1,128)S(1)} %get-tuple-element.36), channel_id=1, source_target_pairs={{4,0},{8,4},{12,8},{16,12},{20,16},{24,20},{28,24},{5,1},{9,5},{13... | collective-permute-start | bytes 49160 | tf_op jit(solution)/shard_map/ppermute | solution.py:23
  188.0 2.7 %collective-permute-start.7 = (f32[1,4096]{1,0:T(1,128)S(1)}, f32[1,4096]{1,0:T(1,128)S(1)}, u32[]{:S(2)}, u32[]{:S(2)}) collective-permute-start(f32[1,4096]{1,0:T(1,128)S(1)} %get-tuple-element.31), channel_id=1, source_target_pairs={{0,4},{4,8},{8,12},{12,16},{16,20},{20,24},{24,28},{1,5},{5,9},{9,... | collective-permute-start | bytes 49160 | tf_op jit(solution)/shard_map/ppermute | solution.py:20
  190.8 4.1 %collective-permute-start.8 = (f32[1,4096]{1,0:T(1,128)S(1)}, f32[1,4096]{1,0:T(1,128)S(1)}, u32[]{:S(2)}, u32[]{:S(2)}) collective-permute-start(f32[1,4096]{1,0:T(1,128)S(1)} %get-tuple-element.32), channel_id=1, source_target_pairs={{4,0},{8,4},{12,8},{16,12},{20,16},{24,20},{28,24},{5,1},{9,5},{13... | collective-permute-start | bytes 49160 | tf_op jit(solution)/shard_map/ppermute | solution.py:23
  194.9 2.4 multiply_add_fusion
  197.3 2.5 convert_element_type.22
  204.4 2.4 collective-permute-start.10
  209.4 3.4 %collective-permute-done.9 = f32[1,4096]{1,0:T(1,128)S(1)} collective-permute-done((f32[1,4096]{1,0:T(1,128)S(1)}, f32[1,4096]{1,0:T(1,128)S(1)}, u32[]{:S(2)}, u32[]{:S(2)}) %collective-permute-start.9) | collective-permute-done | bytes 16416 | tf_op jit(solution)/shard_map/ppermute | solution.py:20
  219.4 4.8 %collective-permute-start.12 = (f32[1,4096]{1,0:T(1,128)S(1)}, f32[1,4096]{1,0:T(1,128)S(1)}, u32[]{:S(2)}, u32[]{:S(2)}) collective-permute-start(f32[1,4096]{1,0:T(1,128)S(1)} %get-tuple-element.28), channel_id=1, source_target_pairs={{4,0},{8,4},{12,8},{16,12},{20,16},{24,20},{28,24},{5,1},{9,5},{13... | collective-permute-start | bytes 49160 | tf_op jit(solution)/shard_map/ppermute | solution.py:23
  224.2 5.1 %fusion.1 = f32[2,129,4096]{2,1,0:T(8,128)S(1)} fusion(f32[2,128,4096]{2,1,0:T(8,128)S(1)} %copy-done.2, f32[2,1,4096]{2,1,0:T(1,128)S(1)} %get-tuple-element.45, f32[2,1,4096]{2,1,0:T(1,128)S(1)} %get-tuple-element.42, f32[2,1,4096]{2,1,0:T(1,128)S(1)} %get-tuple-element.43, f32[2,128,4096]{2,1,0:T(8,128)} %convert_element_type.22, ...), kind=kLoop, calls=%fused_computation.3 | loop fusion | flops 11624448 | bytes 12746752 | tf_op jit(solution)/shard_map/add | solution.py:41
  230.0 2.2 fusion.33
  232.2 2.6 %fusion.36 = f32[130,4097]{1,0:T(8,128)} fusion(f32[130,4098]{1,0:T(8,128)S(1)} %select_maximum_fusion, f32[130,4098]{1,0:T(8,128)S(1)} %select_maximum_fusion.6), kind=kLoop, calls=%fused_computation.57 | loop fusion | flops 3195660 | bytes 10652200 | tf_op jit(solution)/shard_map/mul | solution.py:57
  234.9 9.2 %maximum_divide_fusion = (f32[128,4096]{1,0:T(8,128)}, f32[128,4096]{1,0:T(8,128)}) fusion(f32[128,4096]{1,0:T(8,128)} %copy-done.5, f32[128,4096]{1,0:T(8,128)} %param.14, f32[130,4097]{1,0:T(8,128)} %fusion.36, f32[129,4098]{1,0:T(8,128)} %fusion.33, f32[128,4096]{1,0:T(8,128)} %copy-done.4), kind=kLoop, calls=%fused_computation.95 | loop fusion | flops 3670016 | bytes 18874368 | tf_op jit(solution)/shard_map/div | solution.py:122
  244.0 5.4 %fusion.11 = f32[2,128,4096]{2,1,0:T(8,128)} fusion(f32[2,128,4096]{2,1,0:T(8,128)S(1)} %copy-done.2, f32[2,128,4097]{2,1,0:T(8,128)S(1)} %multiply_add_fusion, f32[2,129,4096]{2,1,0:T(8,128)S(1)} %fusion.1, f32[2,128,4096]{2,1,0:T(8,128)S(1)} %fusion.38, f32[128,4096]{1,0:T(8,128)} %get-tuple-element.16, f32[128,4096]{1,0:T(8,128)} %get-tuple-element.14), kind=kLoop, calls=%fused_computation.18 | loop fusion | flops 8388608 | bytes 33554432 | tf_op jit(solution)/shard_map/mul | solution.py:122
  (84 shorter events, 37.4 us)
Async XLA Ops:
  7.2 164.1 %all-reduce.10.cloned.1.call-start = ((), (), s32[]{:S(2)}) async-start(), calls=%async_computation | async-start | bytes 4194304 | tf_op jit(solution)/shard_map/psum | solution.py:111
  9.9 49.5 %collective-permute-start.2 = (f32[128,4096]{1,0:T(8,128)S(1)}, f32[128,4096]{1,0:T(8,128)S(1)}, u32[]{:S(2)}, u32[]{:S(2)}) collective-permute-start(f32[128,4096]{1,0:T(8,128)S(1)} %get-tuple-element.22), channel_id=1, source_target_pairs={{1,0},{2,1},{3,2},{5,4},{6,5},{7,6},{9,8},{10,9},{11,10},{13,12},{... | collective-permute-start | bytes 6291464 | tf_op jit(solution)/shard_map/ppermute | solution.py:31
  15.3 44.2 %copy-start.11 = (bf16[2,128,4096]{2,1,0:T(8,128)(2,1)S(1)}, bf16[2,128,4096]{2,1,0:T(8,128)(2,1)}, u32[]{:S(2)}) copy-start(bf16[2,128,4096]{2,1,0:T(8,128)(2,1)} %param.12) | copy-start | bytes 6291460
  15.3 44.2 %copy-start.13 = (f32[128,4096]{1,0:T(8,128)S(1)}, f32[128,4096]{1,0:T(8,128)}, u32[]{:S(2)}) copy-start(f32[128,4096]{1,0:T(8,128)} %param.13) | copy-start | bytes 6291460
  66.3 4.4 %collective-permute-start.1 = (f32[3,2,1,4096]{3,2,1,0:T(1,128)S(1)}, f32[3,2,1,4096]{3,2,1,0:T(1,128)S(1)}, u32[]{:S(2)}, u32[]{:S(2)}) collective-permute-start(f32[3,2,1,4096]{3,2,1,0:T(1,128)S(1)} %get-tuple-element.39), channel_id=1, source_target_pairs={{4,0},{8,4},{12,8},{16,12},{20,16},{24,20},{28,24},{5,1},{9,5},{13... | collective-permute-start | bytes 294920 | tf_op jit(solution)/shard_map/ppermute | solution.py:23
  68.2 6.8 %collective-permute-start = (f32[3,2,1,4096]{3,2,1,0:T(1,128)S(1)}, f32[3,2,1,4096]{3,2,1,0:T(1,128)S(1)}, u32[]{:S(2)}, u32[]{:S(2)}) collective-permute-start(f32[3,2,1,4096]{3,2,1,0:T(1,128)S(1)} %get-tuple-element.40), channel_id=1, source_target_pairs={{0,4},{4,8},{8,12},{12,16},{16,20},{20,24},{24,28},{1,5},{5,9},{9,... | collective-permute-start | bytes 294920 | tf_op jit(solution)/shard_map/ppermute | solution.py:20
  75.1 8.3 %copy-start.1 = (f32[2,128,4096]{2,1,0:T(8,128)S(1)}, f32[2,128,4096]{2,1,0:T(8,128)}, u32[]{:S(2)}) copy-start(f32[2,128,4096]{2,1,0:T(8,128)} %param.10) | copy-start | bytes 12582916
  75.1 8.3 %copy-start.14 = (f32[128,4096]{1,0:T(8,128)S(1)}, f32[128,4096]{1,0:T(8,128)}, u32[]{:S(2)}) copy-start(f32[128,4096]{1,0:T(8,128)} %param.13) | copy-start | bytes 6291460
  85.3 9.8 %copy-start.12 = (bf16[2,128,4096]{2,1,0:T(8,128)(2,1)S(1)}, bf16[2,128,4096]{2,1,0:T(8,128)(2,1)}, u32[]{:S(2)}) copy-start(bf16[2,128,4096]{2,1,0:T(8,128)(2,1)} %param.12) | copy-start | bytes 6291460
  88.6 93.3 %collective-permute-start.5 = (f32[1,4096]{1,0:T(1,128)S(1)}, f32[1,4096]{1,0:T(1,128)S(1)}, u32[]{:S(2)}, u32[]{:S(2)}) collective-permute-start(f32[1,4096]{1,0:T(1,128)S(1)} %get-tuple-element.33), channel_id=1, source_target_pairs={{0,4},{4,8},{8,12},{12,16},{16,20},{20,24},{24,28},{1,5},{5,9},{9,... | collective-permute-start | bytes 49160 | tf_op jit(solution)/shard_map/ppermute | solution.py:20
  90.6 91.4 %collective-permute-start.6 = (f32[1,4096]{1,0:T(1,128)S(1)}, f32[1,4096]{1,0:T(1,128)S(1)}, u32[]{:S(2)}, u32[]{:S(2)}) collective-permute-start(f32[1,4096]{1,0:T(1,128)S(1)} %get-tuple-element.34), channel_id=1, source_target_pairs={{4,0},{8,4},{12,8},{16,12},{20,16},{24,20},{28,24},{5,1},{9,5},{13... | collective-permute-start | bytes 49160 | tf_op jit(solution)/shard_map/ppermute | solution.py:23
  171.2 10.7 %copy-start.10 = (f32[128,4096]{1,0:T(8,128)S(1)}, f32[128,4096]{1,0:T(8,128)}, u32[]{:S(2)}) copy-start(f32[128,4096]{1,0:T(8,128)} %copy-done.9) | copy-start | bytes 6291460
  175.5 7.2 %collective-permute-start.3 = (f32[1,4096]{1,0:T(1,128)S(1)}, f32[1,4096]{1,0:T(1,128)S(1)}, u32[]{:S(2)}, u32[]{:S(2)}) collective-permute-start(f32[1,4096]{1,0:T(1,128)S(1)} %get-tuple-element.35), channel_id=1, source_target_pairs={{0,4},{4,8},{8,12},{12,16},{16,20},{20,24},{24,28},{1,5},{5,9},{9,... | collective-permute-start | bytes 49160 | tf_op jit(solution)/shard_map/ppermute | solution.py:20
  177.4 6.0 %collective-permute-start.4 = (f32[1,4096]{1,0:T(1,128)S(1)}, f32[1,4096]{1,0:T(1,128)S(1)}, u32[]{:S(2)}, u32[]{:S(2)}) collective-permute-start(f32[1,4096]{1,0:T(1,128)S(1)} %get-tuple-element.36), channel_id=1, source_target_pairs={{4,0},{8,4},{12,8},{16,12},{20,16},{24,20},{28,24},{5,1},{9,5},{13... | collective-permute-start | bytes 49160 | tf_op jit(solution)/shard_map/ppermute | solution.py:23
  186.2 8.7 %copy-start.2 = (f32[2,128,4096]{2,1,0:T(8,128)S(1)}, f32[2,128,4096]{2,1,0:T(8,128)}, u32[]{:S(2)}) copy-start(f32[2,128,4096]{2,1,0:T(8,128)} %param.10) | copy-start | bytes 12582916
  186.2 8.7 %copy-start.7 = (f32[2,128,4096]{2,1,0:T(8,128)S(1)}, f32[2,128,4096]{2,1,0:T(8,128)}, u32[]{:S(2)}) copy-start(f32[2,128,4096]{2,1,0:T(8,128)} %convert_element_type.23) | copy-start | bytes 12582916
  188.0 11.7 %collective-permute-start.7 = (f32[1,4096]{1,0:T(1,128)S(1)}, f32[1,4096]{1,0:T(1,128)S(1)}, u32[]{:S(2)}, u32[]{:S(2)}) collective-permute-start(f32[1,4096]{1,0:T(1,128)S(1)} %get-tuple-element.31), channel_id=1, source_target_pairs={{0,4},{4,8},{8,12},{12,16},{16,20},{20,24},{24,28},{1,5},{5,9},{9,... | collective-permute-start | bytes 49160 | tf_op jit(solution)/shard_map/ppermute | solution.py:20
  190.8 9.0 %collective-permute-start.8 = (f32[1,4096]{1,0:T(1,128)S(1)}, f32[1,4096]{1,0:T(1,128)S(1)}, u32[]{:S(2)}, u32[]{:S(2)}) collective-permute-start(f32[1,4096]{1,0:T(1,128)S(1)} %get-tuple-element.32), channel_id=1, source_target_pairs={{4,0},{8,4},{12,8},{16,12},{20,16},{24,20},{28,24},{5,1},{9,5},{13... | collective-permute-start | bytes 49160 | tf_op jit(solution)/shard_map/ppermute | solution.py:23
  202.6 6.2 %copy-start.3 = (f32[2,128,4096]{2,1,0:T(8,128)S(1)}, f32[2,128,4096]{2,1,0:T(8,128)}, u32[]{:S(2)}) copy-start(f32[2,128,4096]{2,1,0:T(8,128)} %get-tuple-element.20) | copy-start | bytes 12582916
  204.4 5.0 %collective-permute-start.10 = (f32[1,4096]{1,0:T(1,128)S(1)}, f32[1,4096]{1,0:T(1,128)S(1)}, u32[]{:S(2)}, u32[]{:S(2)}) collective-permute-start(f32[1,4096]{1,0:T(1,128)S(1)} %get-tuple-element.30), channel_id=1, source_target_pairs={{4,0},{8,4},{12,8},{16,12},{20,16},{24,20},{28,24},{5,1},{9,5},{13... | collective-permute-start | bytes 49160 | tf_op jit(solution)/shard_map/ppermute | solution.py:23
  206.8 6.0 %collective-permute-start.9 = (f32[1,4096]{1,0:T(1,128)S(1)}, f32[1,4096]{1,0:T(1,128)S(1)}, u32[]{:S(2)}, u32[]{:S(2)}) collective-permute-start(f32[1,4096]{1,0:T(1,128)S(1)} %get-tuple-element.29), channel_id=1, source_target_pairs={{0,4},{4,8},{8,12},{12,16},{16,20},{20,24},{24,28},{1,5},{5,9},{9,... | collective-permute-start | bytes 49160 | tf_op jit(solution)/shard_map/ppermute | solution.py:20
  217.4 11.9 %copy-start.4 = (f32[128,4096]{1,0:T(8,128)}, f32[128,4096]{1,0:T(8,128)S(1)}, u32[]{:S(2)}) copy-start(f32[128,4096]{1,0:T(8,128)S(1)} %slice_add_fusion.2) | copy-start | bytes 6291460
  217.5 11.8 %collective-permute-start.11 = (f32[1,4096]{1,0:T(1,128)S(1)}, f32[1,4096]{1,0:T(1,128)S(1)}, u32[]{:S(2)}, u32[]{:S(2)}) collective-permute-start(f32[1,4096]{1,0:T(1,128)S(1)} %get-tuple-element.27), channel_id=1, source_target_pairs={{0,4},{4,8},{8,12},{12,16},{16,20},{20,24},{24,28},{1,5},{5,9},{9,... | collective-permute-start | bytes 49160 | tf_op jit(solution)/shard_map/ppermute | solution.py:20
  219.4 9.9 %collective-permute-start.12 = (f32[1,4096]{1,0:T(1,128)S(1)}, f32[1,4096]{1,0:T(1,128)S(1)}, u32[]{:S(2)}, u32[]{:S(2)}) collective-permute-start(f32[1,4096]{1,0:T(1,128)S(1)} %get-tuple-element.28), channel_id=1, source_target_pairs={{4,0},{8,4},{12,8},{16,12},{20,16},{24,20},{28,24},{5,1},{9,5},{13... | collective-permute-start | bytes 49160 | tf_op jit(solution)/shard_map/ppermute | solution.py:23
  (7 other events, 24.3 us)
Sparse Core Ops, SparseCore 0:
  85.4 85.7 all-reduce.9
where the time goes:
time: 257 us; the launch traced here: 256 us
  waiting for transfers between devices  125 us (49%)
  other arithmetic  72.3 us (28%)
  starting transfers between devices  36.6 us (14%)
  between operations  14.6 us (6%)
  local copies, waits for them, and re-layouts  8.08 us (3%)
    psum x1, waiting for transfers between devices, body(): summed_flux = lax.psum(bed_change, 'layer')  73.6 us
    ppermute x1, waiting for transfers between devices, passed_along(): return lax.ppermute(block, axis, route)  42.6 us
    ppermute x6, starting transfers between devices, padded(): lax.ppermute(lax.slice_in_dim(block, 0, width, axis=dim), axis, backward)  22.2 us
    ppermute x6, starting transfers between devices, padded(): lax.ppermute(lax.slice_in_dim(block, block.shape[dim] - width, None, axis...  12.8 us
    div x1, other arithmetic, body(): return (settled * (water_depth / new_depth), height)  9.16 us
    reduce_sum x1, other arithmetic, body(): jnp.sum(spread, 0)  8.31 us
    ppermute x6, waiting for transfers between devices, padded(): lax.ppermute(lax.slice_in_dim(block, block.shape[dim] - width, None, axis...  7.76 us
    add x2, other arithmetic, face_divergence(): jnp.maximum(face_speed, 0.0) * left_val  7.51 us
  transfers between devices with their start and end apart: 14, of which 5 were waited for; matrix products, arithmetic and copies ran while one was open for 9% of the time, Pallas kernels for 0%

commit v1 on v0

--- a/solution.py
+++ b/solution.py
@@ -108,7 +108,7 @@
     bed_change = FLUX_GAIN * jnp.sum(spread, 0) - bottom_flag * settling * concentration[0]
     wet_float = wet_mask.astype(jnp.float32)
     rim_width, rounds = (1, SWEEPS)
-    summed_flux = lax.psum(bed_change, "layer")
+    summed_flux = jnp.sum(lax.all_gather(bed_change, "layer"), axis=0)
     height = bed_level - POROSITY_GAIN * wet_float * (summed_flux + erosion)
     side_pad = ((0, 0), (rim_width, rim_width))
     wet_wide = jnp.pad(padded(wet_float, (("bed", 0),), rim_width), side_pad)

time: 257 us -> 325 us (1.26)
  waiting for transfers between devices: 125 us -> 188 us
  other arithmetic: 72.3 us -> 78.1 us
    all_gather x0 -> x1, waiting for transfers between devices: none -> 137 us  [body(): summed_flux = jnp.sum(lax.all_gather(bed_change, 'layer'), axis=0)]
    psum x1 -> x0, waiting for transfers between devices: 73.6 us -> none  [body(): summed_flux = lax.psum(bed_change, 'layer')]
    reduce_sum x0 -> x1, other arithmetic: none -> 5.54 us  [body(): summed_flux = jnp.sum(lax.all_gather(bed_change, 'layer'), axis=0)]
where the time goes in v1:
time: 325 us
  waiting for transfers between devices  188 us (58%)
  other arithmetic  78.1 us (24%)
  starting transfers between devices  36.6 us (11%)
  between operations  14.6 us (4%)
  local copies, waits for them, and re-layouts  7.94 us (2%)
    all_gather x1, waiting for transfers between devices, body(): summed_flux = jnp.sum(lax.all_gather(bed_change, 'layer'), axis=0)  137 us
    ppermute x1, waiting for transfers between devices, passed_along(): return lax.ppermute(block, axis, route)  42.7 us
    ppermute x6, starting transfers between devices, padded(): lax.ppermute(lax.slice_in_dim(block, 0, width, axis=dim), axis, backward)  22 us
    ppermute x6, starting transfers between devices, padded(): lax.ppermute(lax.slice_in_dim(block, block.shape[dim] - width, None, axis...  13.1 us
    div x1, other arithmetic, body(): return (settled * (water_depth / new_depth), height)  9.16 us
    reduce_sum x1, other arithmetic, body(): jnp.sum(spread, 0)  8.48 us
    add x2, other arithmetic, face_divergence(): jnp.maximum(face_speed, 0.0) * left_val  7.76 us
    ppermute x6, waiting for transfers between devices, padded(): lax.ppermute(lax.slice_in_dim(block, block.shape[dim] - width, None, axis...  7.54 us
  transfers between devices with their start and end apart: 14, of which 5 were waited for; matrix products, arithmetic and copies ran while one was open for 9% of the time, Pallas kernels for 0%

profile of v1, /device:TPU:4, one launch (start us, length us, event | category | flops | bytes accessed | tf_op | source)
XLA Modules:
  0.0 324.8 jit_solution(6414915394457341020)
XLA Ops:
  7.2 2.7 fusion.39
  11.9 3.3 %broadcast_divide_fusion = (f32[128,4096]{1,0:T(8,128)}, f32[128,4096]{1,0:T(8,128)S(1)}) fusion(f32[128,4096]{1,0:T(8,128)} %param.14, f32[128,4096]{1,0:T(8,128)S(1)} %copy-done.16), kind=kLoop, calls=%fused_computation.99 | loop fusion | flops 1048576 | bytes 8388608 | tf_op jit(solution)/shard_map/div | solution.py:103
  16.7 42.7 %collective-permute-done.2 = f32[128,4096]{1,0:T(8,128)S(1)} collective-permute-done((f32[128,4096]{1,0:T(8,128)S(1)}, f32[128,4096]{1,0:T(8,128)S(1)}, u32[]{:S(2)}, u32[]{:S(2)}) %collective-permute-start.2) | collective-permute-done | bytes 2097184 | tf_op jit(solution)/shard_map/ppermute | solution.py:31
  59.5 4.4 %multiply_multiply_fusion = (f32[2,128,4096]{2,1,0:T(8,128)}, f32[2,128,4096]{2,1,0:T(8,128)S(1)}, f32[2,128,4096]{2,1,0:T(8,128)}) fusion(f32[2,128,4096]{2,1,0:T(8,128)S(1)} %copy-done, f32[128,4096]{1,0:T(8,128)S(1)} %broadcast_multiply_fusion, bf16[2,128,4096]{2,1,0:T(8,128)(2,1)S(1)} %copy-done.11, bf16[2,128,4096]{2,1,0:T(8,128)(2,1)S(1)} %copy-done.8, ...), kind=kLoop, calls=%fused_computation.22 | loop fusion | flops 10485760 | bytes 29360128 | tf_op jit(solution)/shard_map/mul | solution.py:86
  68.1 2.4 collective-permute-start
  70.6 4.4 %collective-permute-done = f32[3,2,1,4096]{3,2,1,0:T(1,128)S(1)} collective-permute-done((f32[3,2,1,4096]{3,2,1,0:T(1,128)S(1)}, f32[3,2,1,4096]{3,2,1,0:T(1,128)S(1)}, u32[]{:S(2)}, u32[]{:S(2)}) %collective-permute-start) | collective-permute-done | bytes 98336 | tf_op jit(solution)/shard_map/ppermute | solution.py:20
  75.0 8.5 %fusion.6 = f32[128,4096]{1,0:T(8,128)S(1)} fusion(f32[2,128,4096]{2,1,0:T(8,128)} %copy-done.6, f32[2,1,4096]{2,1,0:T(1,128)S(1)} %get-tuple-element.44, f32[2,1,4096]{2,1,0:T(1,128)S(1)} %get-tuple-element.41, f32[2,128,4096]{2,1,0:T(8,128)} %get-tuple-element.18), kind=kLoop, calls=%fused_computation.11 | loop fusion | flops 6815744 | bytes 10551296 | tf_op jit(solution)/shard_map/reduce_sum | solution.py:108
  90.5 4.5 %collective-permute-start.6 = (f32[1,4096]{1,0:T(1,128)S(1)}, f32[1,4096]{1,0:T(1,128)S(1)}, u32[]{:S(2)}, u32[]{:S(2)}) collective-permute-start(f32[1,4096]{1,0:T(1,128)S(1)} %get-tuple-element.34), channel_id=1, source_target_pairs={{4,0},{8,4},{12,8},{16,12},{20,16},{24,20},{28,24},{5,1},{9,5},{13... | collective-permute-start | bytes 49160 | tf_op jit(solution)/shard_map/ppermute | solution.py:23
  95.1 2.5 convert_element_type.23
  97.6 136.8 %all-gather.3.cloned.1.call-done = f32[512,4096]{1,0:T(8,128)} async-done(((f32[128,4096]{1,0:T(8,128)}), f32[512,4096]{1,0:T(8,128)}) %all-gather.3.cloned.1.call-update) | async-done | bytes 8388624 | tf_op jit(solution)/shard_map/all_gather | solution.py:111
  234.4 5.5 %reduce_sum.19 = f32[128,4096]{1,0:T(8,128)} reduce(f32[4,128,4096]{2,1,0:T(8,128)} %bitcast.26, f32[]{:T(128)} %constant.49.clone.1), dimensions={0}, to_apply=%region_1.2 | reduce | flops 1572864 | bytes 10485764 | tf_op jit(solution)/shard_map/reduce_sum | solution.py:111
  239.9 4.2 %multiply_subtract_fusion = f32[128,4096]{1,0:T(8,128)S(1)} fusion(f32[128,4096]{1,0:T(8,128)} %param.15, f32[128,4096]{1,0:T(8,128)} %reduce_sum.19, f32[128,4096]{1,0:T(8,128)} %param.16, s32[128,4096]{1,0:T(8,128)} %param.17), kind=kLoop, calls=%fused_computation.96 | loop fusion | flops 2621440 | bytes 10485760 | tf_op jit(solution)/shard_map/sub | solution.py:112
  246.2 4.7 %collective-permute-start.4 = (f32[1,4096]{1,0:T(1,128)S(1)}, f32[1,4096]{1,0:T(1,128)S(1)}, u32[]{:S(2)}, u32[]{:S(2)}) collective-permute-start(f32[1,4096]{1,0:T(1,128)S(1)} %get-tuple-element.36), channel_id=1, source_target_pairs={{4,0},{8,4},{12,8},{16,12},{20,16},{24,20},{28,24},{5,1},{9,5},{13... | collective-permute-start | bytes 49160 | tf_op jit(solution)/shard_map/ppermute | solution.py:23
  256.7 2.7 collective-permute-start.7
  259.4 3.9 %collective-permute-start.8 = (f32[1,4096]{1,0:T(1,128)S(1)}, f32[1,4096]{1,0:T(1,128)S(1)}, u32[]{:S(2)}, u32[]{:S(2)}) collective-permute-start(f32[1,4096]{1,0:T(1,128)S(1)} %get-tuple-element.32), channel_id=1, source_target_pairs={{4,0},{8,4},{12,8},{16,12},{20,16},{24,20},{28,24},{5,1},{9,5},{13... | collective-permute-start | bytes 49160 | tf_op jit(solution)/shard_map/ppermute | solution.py:23
  263.4 2.4 multiply_add_fusion
  265.8 2.5 convert_element_type.22
  272.9 2.4 collective-permute-start.10
  278.2 3.1 collective-permute-done.9
  287.9 4.5 %collective-permute-start.12 = (f32[1,4096]{1,0:T(1,128)S(1)}, f32[1,4096]{1,0:T(1,128)S(1)}, u32[]{:S(2)}, u32[]{:S(2)}) collective-permute-start(f32[1,4096]{1,0:T(1,128)S(1)} %get-tuple-element.28), channel_id=1, source_target_pairs={{4,0},{8,4},{12,8},{16,12},{20,16},{24,20},{28,24},{5,1},{9,5},{13... | collective-permute-start | bytes 49160 | tf_op jit(solution)/shard_map/ppermute | solution.py:23
  292.5 5.4 %fusion.1 = f32[2,129,4096]{2,1,0:T(8,128)S(1)} fusion(f32[2,128,4096]{2,1,0:T(8,128)S(1)} %copy-done.2, f32[2,1,4096]{2,1,0:T(1,128)S(1)} %get-tuple-element.45, f32[2,1,4096]{2,1,0:T(1,128)S(1)} %get-tuple-element.42, f32[2,1,4096]{2,1,0:T(1,128)S(1)} %get-tuple-element.43, f32[2,128,4096]{2,1,0:T(8,128)} %convert_element_type.22, ...), kind=kLoop, calls=%fused_computation.3 | loop fusion | flops 11624448 | bytes 12746752 | tf_op jit(solution)/shard_map/add | solution.py:41
  300.8 2.6 fusion.36
  303.4 9.2 %maximum_divide_fusion = (f32[128,4096]{1,0:T(8,128)}, f32[128,4096]{1,0:T(8,128)}) fusion(f32[128,4096]{1,0:T(8,128)} %copy-done.5, f32[128,4096]{1,0:T(8,128)} %param.14, f32[130,4097]{1,0:T(8,128)} %fusion.36, f32[129,4098]{1,0:T(8,128)} %fusion.33, f32[128,4096]{1,0:T(8,128)} %copy-done.4), kind=kLoop, calls=%fused_computation.95 | loop fusion | flops 3670016 | bytes 18874368 | tf_op jit(solution)/shard_map/div | solution.py:122
  312.6 5.4 %fusion.11 = f32[2,128,4096]{2,1,0:T(8,128)} fusion(f32[2,128,4096]{2,1,0:T(8,128)S(1)} %copy-done.2, f32[2,128,4097]{2,1,0:T(8,128)S(1)} %multiply_add_fusion, f32[2,129,4096]{2,1,0:T(8,128)S(1)} %fusion.1, f32[2,128,4096]{2,1,0:T(8,128)S(1)} %fusion.38, f32[128,4096]{1,0:T(8,128)} %get-tuple-element.16, f32[128,4096]{1,0:T(8,128)} %get-tuple-element.14), kind=kLoop, calls=%fused_computation.18 | loop fusion | flops 8388608 | bytes 33554432 | tf_op jit(solution)/shard_map/mul | solution.py:122
  (85 shorter events, 39.4 us)
Async XLA Ops:
  7.2 227.2 %all-gather.3.cloned.1.call-start = ((), (), s32[]{:S(2)}) async-start(), calls=%async_computation | async-start | bytes 10485760 | tf_op jit(solution)/shard_map/all_gather | solution.py:111
  9.9 49.5 %collective-permute-start.2 = (f32[128,4096]{1,0:T(8,128)S(1)}, f32[128,4096]{1,0:T(8,128)S(1)}, u32[]{:S(2)}, u32[]{:S(2)}) collective-permute-start(f32[128,4096]{1,0:T(8,128)S(1)} %get-tuple-element.22), channel_id=1, source_target_pairs={{1,0},{2,1},{3,2},{5,4},{6,5},{7,6},{9,8},{10,9},{11,10},{13,12},{... | collective-permute-start | bytes 6291464 | tf_op jit(solution)/shard_map/ppermute | solution.py:31
  15.2 44.2 %copy-start.11 = (bf16[2,128,4096]{2,1,0:T(8,128)(2,1)S(1)}, bf16[2,128,4096]{2,1,0:T(8,128)(2,1)}, u32[]{:S(2)}) copy-start(bf16[2,128,4096]{2,1,0:T(8,128)(2,1)} %param.12) | copy-start | bytes 6291460
  15.2 44.2 %copy-start.13 = (f32[128,4096]{1,0:T(8,128)S(1)}, f32[128,4096]{1,0:T(8,128)}, u32[]{:S(2)}) copy-start(f32[128,4096]{1,0:T(8,128)} %param.13) | copy-start | bytes 6291460
  66.2 4.4 %collective-permute-start.1 = (f32[3,2,1,4096]{3,2,1,0:T(1,128)S(1)}, f32[3,2,1,4096]{3,2,1,0:T(1,128)S(1)}, u32[]{:S(2)}, u32[]{:S(2)}) collective-permute-start(f32[3,2,1,4096]{3,2,1,0:T(1,128)S(1)} %get-tuple-element.39), channel_id=1, source_target_pairs={{4,0},{8,4},{12,8},{16,12},{20,16},{24,20},{28,24},{5,1},{9,5},{13... | collective-permute-start | bytes 294920 | tf_op jit(solution)/shard_map/ppermute | solution.py:23
  68.1 6.8 %collective-permute-start = (f32[3,2,1,4096]{3,2,1,0:T(1,128)S(1)}, f32[3,2,1,4096]{3,2,1,0:T(1,128)S(1)}, u32[]{:S(2)}, u32[]{:S(2)}) collective-permute-start(f32[3,2,1,4096]{3,2,1,0:T(1,128)S(1)} %get-tuple-element.40), channel_id=1, source_target_pairs={{0,4},{4,8},{8,12},{12,16},{16,20},{20,24},{24,28},{1,5},{5,9},{9,... | collective-permute-start | bytes 294920 | tf_op jit(solution)/shard_map/ppermute | solution.py:20
  75.0 8.5 %copy-start.1 = (f32[2,128,4096]{2,1,0:T(8,128)S(1)}, f32[2,128,4096]{2,1,0:T(8,128)}, u32[]{:S(2)}) copy-start(f32[2,128,4096]{2,1,0:T(8,128)} %param.10) | copy-start | bytes 12582916
  75.0 8.5 %copy-start.14 = (f32[128,4096]{1,0:T(8,128)S(1)}, f32[128,4096]{1,0:T(8,128)}, u32[]{:S(2)}) copy-start(f32[128,4096]{1,0:T(8,128)} %param.13) | copy-start | bytes 6291460
  85.3 9.7 %copy-start.12 = (bf16[2,128,4096]{2,1,0:T(8,128)(2,1)S(1)}, bf16[2,128,4096]{2,1,0:T(8,128)(2,1)}, u32[]{:S(2)}) copy-start(bf16[2,128,4096]{2,1,0:T(8,128)(2,1)} %param.12) | copy-start | bytes 6291460
  88.6 162.3 %collective-permute-start.5 = (f32[1,4096]{1,0:T(1,128)S(1)}, f32[1,4096]{1,0:T(1,128)S(1)}, u32[]{:S(2)}, u32[]{:S(2)}) collective-permute-start(f32[1,4096]{1,0:T(1,128)S(1)} %get-tuple-element.33), channel_id=1, source_target_pairs={{0,4},{4,8},{8,12},{12,16},{16,20},{20,24},{24,28},{1,5},{5,9},{9,... | collective-permute-start | bytes 49160 | tf_op jit(solution)/shard_map/ppermute | solution.py:20
  90.5 160.4 %collective-permute-start.6 = (f32[1,4096]{1,0:T(1,128)S(1)}, f32[1,4096]{1,0:T(1,128)S(1)}, u32[]{:S(2)}, u32[]{:S(2)}) collective-permute-start(f32[1,4096]{1,0:T(1,128)S(1)} %get-tuple-element.34), channel_id=1, source_target_pairs={{4,0},{8,4},{12,8},{16,12},{20,16},{24,20},{28,24},{5,1},{9,5},{13... | collective-permute-start | bytes 49160 | tf_op jit(solution)/shard_map/ppermute | solution.py:23
  239.9 10.9 %copy-start.10 = (f32[128,4096]{1,0:T(8,128)S(1)}, f32[128,4096]{1,0:T(8,128)}, u32[]{:S(2)}) copy-start(f32[128,4096]{1,0:T(8,128)} %copy-done.9) | copy-start | bytes 6291460
  244.2 7.4 %collective-permute-start.3 = (f32[1,4096]{1,0:T(1,128)S(1)}, f32[1,4096]{1,0:T(1,128)S(1)}, u32[]{:S(2)}, u32[]{:S(2)}) collective-permute-start(f32[1,4096]{1,0:T(1,128)S(1)} %get-tuple-element.35), channel_id=1, source_target_pairs={{0,4},{4,8},{8,12},{12,16},{16,20},{20,24},{24,28},{1,5},{5,9},{9,... | collective-permute-start | bytes 49160 | tf_op jit(solution)/shard_map/ppermute | solution.py:20
  246.2 5.9 %collective-permute-start.4 = (f32[1,4096]{1,0:T(1,128)S(1)}, f32[1,4096]{1,0:T(1,128)S(1)}, u32[]{:S(2)}, u32[]{:S(2)}) collective-permute-start(f32[1,4096]{1,0:T(1,128)S(1)} %get-tuple-element.36), channel_id=1, source_target_pairs={{4,0},{8,4},{12,8},{16,12},{20,16},{24,20},{28,24},{5,1},{9,5},{13... | collective-permute-start | bytes 49160 | tf_op jit(solution)/shard_map/ppermute | solution.py:23
  254.9 8.5 %copy-start.2 = (f32[2,128,4096]{2,1,0:T(8,128)S(1)}, f32[2,128,4096]{2,1,0:T(8,128)}, u32[]{:S(2)}) copy-start(f32[2,128,4096]{2,1,0:T(8,128)} %param.10) | copy-start | bytes 12582916
  254.9 8.5 %copy-start.7 = (f32[2,128,4096]{2,1,0:T(8,128)S(1)}, f32[2,128,4096]{2,1,0:T(8,128)}, u32[]{:S(2)}) copy-start(f32[2,128,4096]{2,1,0:T(8,128)} %convert_element_type.23) | copy-start | bytes 12582916
  256.7 11.6 %collective-permute-start.7 = (f32[1,4096]{1,0:T(1,128)S(1)}, f32[1,4096]{1,0:T(1,128)S(1)}, u32[]{:S(2)}, u32[]{:S(2)}) collective-permute-start(f32[1,4096]{1,0:T(1,128)S(1)} %get-tuple-element.31), channel_id=1, source_target_pairs={{0,4},{4,8},{8,12},{12,16},{16,20},{20,24},{24,28},{1,5},{5,9},{9,... | collective-permute-start | bytes 49160 | tf_op jit(solution)/shard_map/ppermute | solution.py:20
  259.4 8.8 %collective-permute-start.8 = (f32[1,4096]{1,0:T(1,128)S(1)}, f32[1,4096]{1,0:T(1,128)S(1)}, u32[]{:S(2)}, u32[]{:S(2)}) collective-permute-start(f32[1,4096]{1,0:T(1,128)S(1)} %get-tuple-element.32), channel_id=1, source_target_pairs={{4,0},{8,4},{12,8},{16,12},{20,16},{24,20},{28,24},{5,1},{9,5},{13... | collective-permute-start | bytes 49160 | tf_op jit(solution)/shard_map/ppermute | solution.py:23
  271.1 6.4 %copy-start.3 = (f32[2,128,4096]{2,1,0:T(8,128)S(1)}, f32[2,128,4096]{2,1,0:T(8,128)}, u32[]{:S(2)}) copy-start(f32[2,128,4096]{2,1,0:T(8,128)} %get-tuple-element.20) | copy-start | bytes 12582916
  272.9 5.2 %collective-permute-start.10 = (f32[1,4096]{1,0:T(1,128)S(1)}, f32[1,4096]{1,0:T(1,128)S(1)}, u32[]{:S(2)}, u32[]{:S(2)}) collective-permute-start(f32[1,4096]{1,0:T(1,128)S(1)} %get-tuple-element.30), channel_id=1, source_target_pairs={{4,0},{8,4},{12,8},{16,12},{20,16},{24,20},{28,24},{5,1},{9,5},{13... | collective-permute-start | bytes 49160 | tf_op jit(solution)/shard_map/ppermute | solution.py:23
  275.3 6.0 %collective-permute-start.9 = (f32[1,4096]{1,0:T(1,128)S(1)}, f32[1,4096]{1,0:T(1,128)S(1)}, u32[]{:S(2)}, u32[]{:S(2)}) collective-permute-start(f32[1,4096]{1,0:T(1,128)S(1)} %get-tuple-element.29), channel_id=1, source_target_pairs={{0,4},{4,8},{8,12},{12,16},{16,20},{20,24},{24,28},{1,5},{5,9},{9,... | collective-permute-start | bytes 49160 | tf_op jit(solution)/shard_map/ppermute | solution.py:20
  285.9 11.9 %copy-start.4 = (f32[128,4096]{1,0:T(8,128)}, f32[128,4096]{1,0:T(8,128)S(1)}, u32[]{:S(2)}) copy-start(f32[128,4096]{1,0:T(8,128)S(1)} %slice_add_fusion.2) | copy-start | bytes 6291460
  286.0 11.8 %collective-permute-start.11 = (f32[1,4096]{1,0:T(1,128)S(1)}, f32[1,4096]{1,0:T(1,128)S(1)}, u32[]{:S(2)}, u32[]{:S(2)}) collective-permute-start(f32[1,4096]{1,0:T(1,128)S(1)} %get-tuple-element.27), channel_id=1, source_target_pairs={{0,4},{4,8},{8,12},{12,16},{16,20},{20,24},{24,28},{1,5},{5,9},{9,... | collective-permute-start | bytes 49160 | tf_op jit(solution)/shard_map/ppermute | solution.py:20
  287.9 9.9 %collective-permute-start.12 = (f32[1,4096]{1,0:T(1,128)S(1)}, f32[1,4096]{1,0:T(1,128)S(1)}, u32[]{:S(2)}, u32[]{:S(2)}) collective-permute-start(f32[1,4096]{1,0:T(1,128)S(1)} %get-tuple-element.28), channel_id=1, source_target_pairs={{4,0},{8,4},{12,8},{16,12},{20,16},{24,20},{28,24},{5,1},{9,5},{13... | collective-permute-start | bytes 49160 | tf_op jit(solution)/shard_map/ppermute | solution.py:23
  (7 other events, 24.4 us)
Sparse Core Ops, SparseCore 0:
  85.4 148.9 all-gather.2
